TPU v7x, 32 devices: a whole 2x2x4 slice. The times are simulated.
32 devices in a mesh: dp: 8 (over z, y), ctx: 4 (over x, core).
Axes of the slice: x: 2, y: 2, z: 4, core: 2. Of those that a mesh axis runs over, the one named last changes fastest.
Arguments:
- hidden_in: bfloat16 [8192, 1024], P(('dp', 'ctx')), may hold values from -120 to 120
- cotangent: bfloat16 [8192, 1024], P(('dp', 'ctx')), may hold values from -6 to 6
- block_order: int32 [8, 8], P('dp'), may hold values from 0 to 7, each once within a row
- w_query: bfloat16 [2097152], P(('dp', 'ctx')), may hold values from -0.1875 to 0.1875
- key_weight: bfloat16 [1048576], P(('dp', 'ctx')), may hold values from -0.1875 to 0.1875
- value_weight: bfloat16 [1048576], P(('dp', 'ctx')), may hold values from -0.1875 to 0.1875
- w_out: bfloat16 [2097152], P(('dp', 'ctx')), may hold values from -1 to 1
- w_gate: bfloat16 [3145728], P(('dp', 'ctx')), may hold values from -0.1875 to 0.1875
- w_up: bfloat16 [3145728], P(('dp', 'ctx')), may hold values from -0.1875 to 0.1875
- w_down: bfloat16 [3145728], P(('dp', 'ctx')), may hold values from -0.109375 to 0.109375
- norm_gains: bfloat16 [2304], P(('dp', 'ctx')), may hold values from 0.099609375 to 1.8984375
Outputs:
- block_out: bfloat16 [8192, 1024], P(('dp', 'ctx'))
- grad_in: float32 [8192, 1024], P(('dp', 'ctx'))
- grad_query: float32 [2097152], P(('dp', 'ctx'))
- grad_key: float32 [1048576], P(('dp', 'ctx'))
- grad_value: float32 [1048576], P(('dp', 'ctx'))
- grad_out: float32 [2097152], P(('dp', 'ctx'))
- grad_gate: float32 [3145728], P(('dp', 'ctx'))
- grad_up: float32 [3145728], P(('dp', 'ctx'))
- grad_down: float32 [3145728], P(('dp', 'ctx'))
- grad_gains: float32 [2304], P(('dp', 'ctx'))
Inputs may be any that keep to these rules, and one draw needn't show every extreme that they name: Each row is a permutation of 0 to 7; stored block j of sequence s holds positions block_order[s, j] * 128 onward.
All inputs are finite; a program needn't handle non-finite values.
Results may differ from a plain program's by a relative error of at most 0.015.
Values may be sent and summed in bfloat16 or wider, within the bound.
A program may use at most 256 MiB of HBM per device.

v0:
```python
import jax
import jax.numpy as jnp
from jax import lax
from jax.sharding import PartitionSpec as P

QUERY_HEADS = 16
KEY_VALUE_HEADS = 8
HEAD_SIZE = 128
FEEDFORWARD_UNITS = 3072


NORM_EPS = 1e-06
ROPE_THETA = 1000000.0


def rotary_tables(positions):
    half_dim = HEAD_SIZE // 2
    inverse = ROPE_THETA ** (-(jnp.arange(half_dim, dtype=jnp.float32) * 2.0 / HEAD_SIZE))
    angles = positions.astype(jnp.float32)[:, None] * inverse[None, :]
    return (jnp.cos(angles)[:, None, :], jnp.sin(angles)[:, None, :])


def apply_rotary(value_rows, cosine_table, sine_table):
    half_dim = value_rows.shape[-1] // 2
    first_half = value_rows[..., :half_dim]
    second_half = value_rows[..., half_dim:]
    return jnp.concatenate(
        [
            first_half * cosine_table - second_half * sine_table,
            second_half * cosine_table + first_half * sine_table,
        ],
        axis=-1,
    )


def invert_rotary(grads, cosine_table, sine_table):
    half_dim = grads.shape[-1] // 2
    first_half = grads[..., :half_dim]
    second_half = grads[..., half_dim:]
    return jnp.concatenate(
        [
            first_half * cosine_table + second_half * sine_table,
            second_half * cosine_table - first_half * sine_table,
        ],
        axis=-1,
    )


def norm_forward(value_rows, gain):
    inv_root = lax.rsqrt(jnp.mean(value_rows * value_rows, axis=-1, keepdims=True) + NORM_EPS)
    return (value_rows * inv_root * gain, inv_root)


def norm_backward(value_rows, inv_root, gain, upstream):
    weighted = upstream * gain
    return inv_root * weighted - value_rows * inv_root**3 * jnp.mean(
        weighted * value_rows, axis=-1, keepdims=True
    )


def left_contract(left, right):
    return lax.dot_general(
        left, right, (((0,), (0,)), ((), ())), preferred_element_type=jnp.float32
    )


def right_contract(left, right):
    return lax.dot_general(
        left, right, (((1,), (1,)), ((), ())), preferred_element_type=jnp.float32
    )


def attention_scores(query_b, key_gathered, visible, score_scale):
    key_length = key_gathered.shape[0]
    key_rows_fourdim = key_gathered.reshape(key_length, KEY_VALUE_HEADS, HEAD_SIZE)
    scores = (
        jnp.einsum("tkgd,nkd->kgtn", query_b, key_rows_fourdim, preferred_element_type=jnp.float32)
        * score_scale
    )
    return jnp.where(visible[None, None], scores, -1e30)


def shards(
    hidden_in,
    cotangent,
    block_order,
    w_query,
    key_weight,
    value_weight,
    w_out,
    w_gate,
    w_up,
    w_down,
    norm_gains,
):
    token_rows = hidden_in.shape[0]
    width_model = hidden_in.shape[1]
    block_len = token_rows // 2
    query_groups = QUERY_HEADS // KEY_VALUE_HEADS
    query_width = QUERY_HEADS * HEAD_SIZE
    kv_width = KEY_VALUE_HEADS * HEAD_SIZE
    score_scale = HEAD_SIZE ** (-0.5)
    orders = block_order[0]
    key_places = (
        orders[:, None] * block_len + jnp.arange(block_len, dtype=jnp.int32)[None, :]
    ).reshape(-1)
    sequence_length = key_places.shape[0]
    query_places = lax.dynamic_slice_in_dim(
        key_places, lax.axis_index("ctx") * token_rows, token_rows
    )
    visible = key_places[None, :] <= query_places[:, None]
    cosine_table, sine_table = rotary_tables(query_places)
    query_local = w_query.reshape(-1, query_width)
    key_local = key_weight.reshape(-1, kv_width)
    value_local = value_weight.reshape(-1, kv_width)
    out_local = w_out.reshape(-1, width_model)
    gate_local = w_gate.reshape(-1, FEEDFORWARD_UNITS)
    up_local = w_up.reshape(-1, FEEDFORWARD_UNITS)
    down_local = w_down.reshape(-1, width_model)
    gathered = (
        lax.all_gather(query_local, ("dp", "ctx"), axis=0, tiled=True),
        lax.all_gather(key_local, ("dp", "ctx"), axis=0, tiled=True),
        lax.all_gather(value_local, ("dp", "ctx"), axis=0, tiled=True),
        lax.all_gather(out_local, ("dp", "ctx"), axis=0, tiled=True),
        lax.all_gather(norm_gains, ("dp", "ctx"), axis=0, tiled=True),
    )
    attn_set = (gathered[0], gathered[1], gathered[2], gathered[3])
    layer_gains = gathered[4].astype(jnp.float32)
    gain_one = layer_gains[:width_model]
    gain_two = layer_gains[width_model : 2 * width_model]
    query_norm_gain = layer_gains[2 * width_model : 2 * width_model + HEAD_SIZE]
    gain_key = layer_gains[2 * width_model + HEAD_SIZE :]
    inputs = hidden_in.astype(jnp.float32)
    first_normed, scale_one = norm_forward(inputs, gain_one)
    normed_one_b = first_normed.astype(jnp.bfloat16)
    query_raw = jnp.dot(normed_one_b, attn_set[0], preferred_element_type=jnp.float32).reshape(
        token_rows, QUERY_HEADS, HEAD_SIZE
    )
    key_raw = jnp.dot(normed_one_b, attn_set[1], preferred_element_type=jnp.float32).reshape(
        token_rows, KEY_VALUE_HEADS, HEAD_SIZE
    )
    value_b = jnp.dot(normed_one_b, attn_set[2], preferred_element_type=jnp.float32).astype(
        jnp.bfloat16
    )
    query_after_norm, query_scale = norm_forward(query_raw, query_norm_gain)
    key_after_norm, key_scale = norm_forward(key_raw, gain_key)
    query_b = (
        apply_rotary(query_after_norm, cosine_table, sine_table)
        .astype(jnp.bfloat16)
        .reshape(token_rows, KEY_VALUE_HEADS, query_groups, HEAD_SIZE)
    )
    key_block = (
        apply_rotary(key_after_norm, cosine_table, sine_table)
        .astype(jnp.bfloat16)
        .reshape(token_rows, kv_width)
    )
    key_gathered, value_gathered = (
        lax.all_gather(key_block, "ctx", axis=0, tiled=True),
        lax.all_gather(value_b, "ctx", axis=0, tiled=True),
    )
    scores = attention_scores(query_b, key_gathered, visible, score_scale)
    maxima = jnp.max(scores, axis=-1, keepdims=True)
    expo = jnp.exp(scores - maxima)
    totals = jnp.sum(expo, axis=-1, keepdims=True)
    log_total = maxima + jnp.log(totals)
    probs_b = (expo / totals).astype(jnp.bfloat16)
    value_rows_fourdim = value_gathered.reshape(sequence_length, KEY_VALUE_HEADS, HEAD_SIZE)
    mixed_b = (
        jnp.einsum(
            "kgtn,nkd->tkgd", probs_b, value_rows_fourdim, preferred_element_type=jnp.float32
        )
        .reshape(token_rows, query_width)
        .astype(jnp.bfloat16)
    )
    middle = inputs + jnp.dot(mixed_b, attn_set[3], preferred_element_type=jnp.float32)
    normed_two, scale_two = norm_forward(middle, gain_two)
    normed_two_b = normed_two.astype(jnp.bfloat16)
    mlp_set = (
        lax.all_gather(gate_local, ("dp", "ctx"), axis=0, tiled=True),
        lax.all_gather(up_local, ("dp", "ctx"), axis=0, tiled=True),
        lax.all_gather(down_local, ("dp", "ctx"), axis=0, tiled=True),
    )
    gate_act = jnp.dot(normed_two_b, mlp_set[0], preferred_element_type=jnp.float32)
    up_act = jnp.dot(normed_two_b, mlp_set[1], preferred_element_type=jnp.float32)
    sigmoid = jax.nn.sigmoid(gate_act)
    activated = gate_act * sigmoid
    hidden_b = (activated * up_act).astype(jnp.bfloat16)
    result = middle + jnp.dot(hidden_b, mlp_set[2], preferred_element_type=jnp.float32)
    block_out = result.astype(jnp.bfloat16)
    upstream = cotangent.astype(jnp.float32)
    grad_down_full = left_contract(hidden_b, cotangent)
    grad_hidden = right_contract(cotangent, mlp_set[2])
    grad_gate_b = (grad_hidden * up_act * sigmoid * (1.0 + gate_act * (1.0 - sigmoid))).astype(
        jnp.bfloat16
    )
    grad_up_b = (grad_hidden * activated).astype(jnp.bfloat16)
    grad_gate_full = left_contract(normed_two_b, grad_gate_b)
    grad_up_full = left_contract(normed_two_b, grad_up_b)
    grad_normed_two = right_contract(grad_gate_b, mlp_set[0]) + right_contract(
        grad_up_b, mlp_set[1]
    )
    grad_gain_two = jnp.sum(grad_normed_two * middle * scale_two, axis=0)
    grad_middle = upstream + norm_backward(middle, scale_two, gain_two, grad_normed_two)
    mlp_grads = (
        lax.psum_scatter(grad_gate_full, ("dp", "ctx"), scatter_dimension=0, tiled=True),
        lax.psum_scatter(grad_up_full, ("dp", "ctx"), scatter_dimension=0, tiled=True),
        lax.psum_scatter(grad_down_full, ("dp", "ctx"), scatter_dimension=0, tiled=True),
    )
    key_rebuilt, value_rebuilt = (
        lax.all_gather(key_block, "ctx", axis=0, tiled=True),
        lax.all_gather(value_b, "ctx", axis=0, tiled=True),
    )
    grad_proj_b = grad_middle.astype(jnp.bfloat16)
    grad_out_full = left_contract(mixed_b, grad_proj_b)
    grad_mixed_b = (
        right_contract(grad_proj_b, attn_set[3])
        .astype(jnp.bfloat16)
        .reshape(token_rows, KEY_VALUE_HEADS, query_groups, HEAD_SIZE)
    )
    scores_again = attention_scores(query_b, key_rebuilt, visible, score_scale)
    probs = jnp.exp(scores_again - log_total)
    probs_again_b = probs.astype(jnp.bfloat16)
    value_rows_rebuilt = value_rebuilt.reshape(sequence_length, KEY_VALUE_HEADS, HEAD_SIZE)
    key_rows_rebuilt = key_rebuilt.reshape(sequence_length, KEY_VALUE_HEADS, HEAD_SIZE)
    grad_value_all = jnp.einsum(
        "kgtn,tkgd->nkd", probs_again_b, grad_mixed_b, preferred_element_type=jnp.float32
    ).reshape(sequence_length, kv_width)
    grad_probs = jnp.einsum(
        "tkgd,nkd->kgtn", grad_mixed_b, value_rows_rebuilt, preferred_element_type=jnp.float32
    )
    delta = jnp.sum(probs * grad_probs, axis=-1, keepdims=True)
    grad_scores_b = (probs * (grad_probs - delta) * score_scale).astype(jnp.bfloat16)
    grad_query_rot = jnp.einsum(
        "kgtn,nkd->tkgd", grad_scores_b, key_rows_rebuilt, preferred_element_type=jnp.float32
    ).reshape(token_rows, QUERY_HEADS, HEAD_SIZE)
    grad_key_all = jnp.einsum(
        "kgtn,tkgd->nkd", grad_scores_b, query_b, preferred_element_type=jnp.float32
    ).reshape(sequence_length, kv_width)
    key_rotated_gradient, grad_value_local = (
        lax.psum_scatter(
            grad_key_all.astype(jnp.bfloat16), "ctx", scatter_dimension=0, tiled=True
        ).astype(jnp.float32),
        lax.psum_scatter(
            grad_value_all.astype(jnp.bfloat16), "ctx", scatter_dimension=0, tiled=True
        ).astype(jnp.float32),
    )
    grad_query_normed = invert_rotary(grad_query_rot, cosine_table, sine_table)
    key_normed_gradient = invert_rotary(
        key_rotated_gradient.reshape(token_rows, KEY_VALUE_HEADS, HEAD_SIZE),
        cosine_table,
        sine_table,
    )
    grad_gain_query = jnp.sum(grad_query_normed * query_raw * query_scale, axis=(0, 1))
    grad_gain_key = jnp.sum(key_normed_gradient * key_raw * key_scale, axis=(0, 1))
    grad_query_b = (
        norm_backward(query_raw, query_scale, query_norm_gain, grad_query_normed)
        .astype(jnp.bfloat16)
        .reshape(token_rows, query_width)
    )
    grad_key_b = (
        norm_backward(key_raw, key_scale, gain_key, key_normed_gradient)
        .astype(jnp.bfloat16)
        .reshape(token_rows, kv_width)
    )
    grad_value_b = grad_value_local.astype(jnp.bfloat16)
    grad_query_full = left_contract(normed_one_b, grad_query_b)
    grad_key_full = left_contract(normed_one_b, grad_key_b)
    grad_value_full = left_contract(normed_one_b, grad_value_b)
    grad_normed_one = (
        right_contract(grad_query_b, attn_set[0])
        + right_contract(grad_key_b, attn_set[1])
        + right_contract(grad_value_b, attn_set[2])
    )
    grad_gain_one = jnp.sum(grad_normed_one * inputs * scale_one, axis=0)
    grad_in = grad_middle + norm_backward(inputs, scale_one, gain_one, grad_normed_one)
    grad_gain_all = jnp.concatenate([grad_gain_one, grad_gain_two, grad_gain_query, grad_gain_key])
    attn_grads = (
        lax.psum_scatter(grad_query_full, ("dp", "ctx"), scatter_dimension=0, tiled=True),
        lax.psum_scatter(grad_key_full, ("dp", "ctx"), scatter_dimension=0, tiled=True),
        lax.psum_scatter(grad_value_full, ("dp", "ctx"), scatter_dimension=0, tiled=True),
        lax.psum_scatter(grad_out_full, ("dp", "ctx"), scatter_dimension=0, tiled=True),
        lax.psum_scatter(grad_gain_all, ("dp", "ctx"), scatter_dimension=0, tiled=True),
    )
    return (
        block_out,
        grad_in,
        attn_grads[0].reshape(-1),
        attn_grads[1].reshape(-1),
        attn_grads[2].reshape(-1),
        attn_grads[3].reshape(-1),
        mlp_grads[0].reshape(-1),
        mlp_grads[1].reshape(-1),
        mlp_grads[2].reshape(-1),
        attn_grads[4],
    )


def solution(mesh):
    placed = (
        P(("dp", "ctx"), None),
        P(("dp", "ctx"), None),
        P("dp", None),
        P(("dp", "ctx")),
        P(("dp", "ctx")),
        P(("dp", "ctx")),
        P(("dp", "ctx")),
        P(("dp", "ctx")),
        P(("dp", "ctx")),
        P(("dp", "ctx")),
        P(("dp", "ctx")),
    )
    return jax.shard_map(
        shards,
        mesh=mesh,
        in_specs=placed,
        out_specs=(
            P(("dp", "ctx"), None),
            P(("dp", "ctx"), None),
            P(("dp", "ctx")),
            P(("dp", "ctx")),
            P(("dp", "ctx")),
            P(("dp", "ctx")),
            P(("dp", "ctx")),
            P(("dp", "ctx")),
            P(("dp", "ctx")),
            P(("dp", "ctx")),
        ),
        check_vma=False,
    )
```

profile of v0, /device:TPU:0, one launch (start us, length us, event | category | flops | bytes accessed | tf_op | source)
XLA Modules:
  0.0 1686.3 jit_solution(9997706891547744487)
XLA Ops:
  11.4 42.1 %all-reduce = bf16[2304]{0:T(1024)(128)(2,1)S(1)} all-reduce(bf16[2304]{0:T(1024)(128)(2,1)S(1)} %dynamic-update-slice), channel_id=1, replica_groups=mesh['dp'=8,'ctx'=4] {'dp','ctx'}, use_global_device_ids=true, to_apply=%add | all-reduce | flops 2304 | bytes 9216
  55.3 15.3 all-gather.10.cloned.1.call-done
  76.6 52.7 %all-gather.14.cloned.1.call-done = bf16[1024,1024]{1,0:T(8,128)(2,1)} async-done(((bf16[32,1024]{1,0:T(8,128)(2,1)}), bf16[1024,1024]{1,0:T(8,128)(2,1)}) %all-gather.14.cloned.1.call-update) | async-done | bytes 2097168 | tf_op jit(solution)/shard_map/all_gather | solution.py:122
  140.2 12.7 all-gather.12.cloned.1.call-done
  156.4 61.8 %all-gather.18.cloned.1.call-done = bf16[1024,2048]{1,0:T(8,128)(2,1)} async-done(((bf16[32,2048]{1,0:T(8,128)(2,1)}), bf16[1024,2048]{1,0:T(8,128)(2,1)}) %all-gather.18.cloned.1.call-update) | async-done | bytes 4194320 | tf_op jit(solution)/shard_map/all_gather | solution.py:121
  228.1 13.5 all-gather.16.cloned.1.call-done
  241.7 11.7 fusion.67
  261.5 8.9 fusion.24
  270.4 36.6 %all-gather.20.cloned.1.call-done = bf16[2048,1024]{1,0:T(8,128)(2,1)} async-done(((bf16[64,1024]{1,0:T(8,128)(2,1)}), bf16[2048,1024]{1,0:T(8,128)(2,1)}) %all-gather.20.cloned.1.call-update) | async-done | bytes 4194320 | tf_op jit(solution)/shard_map/all_gather | solution.py:124
  312.3 66.3 %all-gather.22.cloned.1.call-done = bf16[1024,3072]{1,0:T(8,128)(2,1)} async-done(((bf16[32,3072]{1,0:T(8,128)(2,1)}), bf16[1024,3072]{1,0:T(8,128)(2,1)}) %all-gather.22.cloned.1.call-update) | async-done | bytes 6291472 | tf_op jit(solution)/shard_map/all_gather | solution.py:179
  384.8 65.2 %all-gather.24.cloned.1.call-done = bf16[1024,3072]{1,0:T(8,128)(2,1)} async-done(((bf16[32,3072]{1,0:T(8,128)(2,1)}), bf16[1024,3072]{1,0:T(8,128)(2,1)}) %all-gather.24.cloned.1.call-update) | async-done | bytes 6291472 | tf_op jit(solution)/shard_map/all_gather | solution.py:180
  456.3 65.3 %all-gather.26.cloned.1.call-done = bf16[3072,1024]{1,0:T(8,128)(2,1)} async-done(((bf16[96,1024]{1,0:T(8,128)(2,1)}), bf16[3072,1024]{1,0:T(8,128)(2,1)}) %all-gather.26.cloned.1.call-update) | async-done | bytes 6291472 | tf_op jit(solution)/shard_map/all_gather | solution.py:181
  545.2 10.3 bitcast_convert_fusion
  555.6 10.4 fusion.22
  566.0 25.9 %bitcast_convert_fusion.1 = bf16[8,128,1024]{2,1,0:T(8,128)(2,1)} fusion(f32[8,1024,256,2]{2,1,3,0:T(8,128)} %fusion.22, f32[8,2,256,1024]{2,3,1,0:T(8,128)} %get-tuple-element.54, f32[8,2,256]{2,1,0:T(2,128)} %bitcast.240, bf16[256,8,2,64]{3,0,2,1:T(8,128)(2,1)} %bitcast.212, bf16[256,8,2,64]{3,0,2,1:T(8,128)(2,1)} %bitcast.210), kind=kOutput, calls=%fused_computation.19 | convolution fusion | flops 1106252800 | bytes 36716544 | tf_op jit(solution)/shard_map/kgtn,tkgd->nkd/dot_general | solution.py:236
  598.0 24.4 %reduce-scatter.10.cloned.1.call-done = bf16[256,1024]{0,1:T(8,128)(2,1)} async-done(((bf16[1024,1024]{0,1:T(8,128)(2,1)}), bf16[256,1024]{0,1:T(8,128)(2,1)}) %reduce-scatter.10.cloned.1.call-update) | async-done | bytes 524304 | tf_op jit(solution)/shard_map/reduce_scatter | solution.py:240
  646.5 25.6 %fusion.12 = f32[8,128,2,256]{3,1,2,0:T(8,128)} fusion(bf16[1024,8,128,1]{0,2,3,1:T(8,128)(2,1)} %bitcast.208, f32[8,1024,256,2]{2,1,3,0:T(8,128)} %fusion.22, f32[8,2,256,1024]{2,3,1,0:T(8,128)} %get-tuple-element.54, f32[8,2,256]{2,1,0:T(2,128)} %bitcast.241), kind=kOutput, calls=%fused_computation.17 | convolution fusion | flops 1103107072 | bytes 37765120 | tf_op jit(solution)/shard_map/kgtn,nkd->tkgd/dot_general | solution.py:233
  741.4 39.6 %all-reduce.1 = f32[2304]{0:T(1024)S(1)} all-reduce(f32[2304]{0:T(1024)S(1)} %pad_maximum_fusion.6), channel_id=11, replica_groups=mesh['dp'=8,'ctx'=4] {'dp','ctx'}, use_global_device_ids=true, to_apply=%region_26.27.clone | all-reduce | flops 2304 | bytes 18432
  784.4 120.4 %reduce-scatter.16.cloned.1.call-done = f32[32,1024]{1,0:T(8,128)} async-done(((f32[1024,1024]{1,0:T(8,128)}), f32[32,1024]{1,0:T(8,128)}) %reduce-scatter.16.cloned.1.call-update) | async-done | bytes 131088 | tf_op jit(solution)/shard_map/reduce_scatter | solution.py:279
  906.3 145.4 %reduce-scatter.14.cloned.1.call-done = f32[32,2048]{1,0:T(8,128)} async-done(((f32[1024,2048]{1,0:T(8,128)}), f32[32,2048]{1,0:T(8,128)}) %reduce-scatter.14.cloned.1.call-update) | async-done | bytes 262160 | tf_op jit(solution)/shard_map/reduce_scatter | solution.py:278
  1053.4 155.5 %reduce-scatter.22.cloned.1.call-done = f32[32,3072]{1,0:T(8,128)} async-done(((f32[1024,3072]{1,0:T(8,128)}), f32[32,3072]{1,0:T(8,128)}) %reduce-scatter.22.cloned.1.call-update) | async-done | bytes 393232 | tf_op jit(solution)/shard_map/reduce_scatter | solution.py:205
  1210.7 159.6 %reduce-scatter.24.cloned.1.call-done = f32[32,3072]{1,0:T(8,128)} async-done(((f32[1024,3072]{1,0:T(8,128)}), f32[32,3072]{1,0:T(8,128)}) %reduce-scatter.24.cloned.1.call-update) | async-done | bytes 393232 | tf_op jit(solution)/shard_map/reduce_scatter | solution.py:206
  1372.1 148.1 %reduce-scatter.20.cloned.1.call-done = f32[64,1024]{1,0:T(8,128)} async-done(((f32[2048,1024]{1,0:T(8,128)}), f32[64,1024]{1,0:T(8,128)}) %reduce-scatter.20.cloned.1.call-update) | async-done | bytes 262160 | tf_op jit(solution)/shard_map/reduce_scatter | solution.py:281
  1521.9 155.5 %reduce-scatter.26.cloned.1.call-done = f32[96,1024]{1,0:T(8,128)} async-done(((f32[3072,1024]{1,0:T(8,128)}), f32[96,1024]{1,0:T(8,128)}) %reduce-scatter.26.cloned.1.call-update) | async-done | bytes 393232 | tf_op jit(solution)/shard_map/reduce_scatter | solution.py:207
  (230 shorter events, 198.5 us)
Async XLA Ops:
  7.2 122.1 %copy-start = (bf16[256,1024]{1,0:T(8,128)(2,1)S(1)}, bf16[256,1024]{1,0:T(8,128)(2,1)}, u32[]{:S(2)}) copy-start(bf16[256,1024]{1,0:T(8,128)(2,1)} %param.11) | copy-start | bytes 1572868
  7.2 66.8 %copy-start.29 = (bf16[65536]{0:T(1024)(128)(2,1)S(1)}, bf16[65536]{0:T(1024)(128)(2,1)}, u32[]{:S(2)}) copy-start(bf16[65536]{0:T(1024)(128)(2,1)} %param.14) | copy-start | bytes 393220
  7.2 67.6 %copy-start.44 = (s32[1,8]{1,0:T(1,128)S(1)}, s32[1,8]{1,0:T(1,128)}, u32[]{:S(2)}) copy-start(s32[1,8]{1,0:T(1,128)} %param.13) | copy-start | bytes 100
  7.2 63.4 %all-gather.10.cloned.1.call-start = ((), (), s32[]{:S(2)}) async-start(), calls=%async_computation.9 | async-start | bytes 2162688 | tf_op jit(solution)/shard_map/all_gather | solution.py:123
  8.8 120.4 %all-gather.14.cloned.1.call-start = ((), (), s32[]{:S(2)}) async-start(), calls=%async_computation.11 | async-start | bytes 2162688 | tf_op jit(solution)/shard_map/all_gather | solution.py:122
  10.4 142.5 %all-gather.12.cloned.1.call-start = ((), (), s32[]{:S(2)}) async-start(), calls=%async_computation.10 | async-start | bytes 2621440 | tf_op jit(solution)/shard_map/all_gather | solution.py:159
  73.9 144.3 %all-gather.18.cloned.1.call-start = ((), (), s32[]{:S(2)}) async-start(), calls=%async_computation.13 | async-start | bytes 4325376 | tf_op jit(solution)/shard_map/all_gather | solution.py:121
  74.7 166.9 %all-gather.16.cloned.1.call-start = ((), (), s32[]{:S(2)}) async-start(), calls=%async_computation.12 | async-start | bytes 2621440 | tf_op jit(solution)/shard_map/all_gather | solution.py:158
  76.1 57.9 %copy-start.36 = (f32[128]{0:T(128)}, f32[128]{0:T(128)S(1)}, u32[]{:S(2)}) copy-start(f32[128]{0:T(128)S(1)} %get-tuple-element.46) | copy-start | bytes 1540
  136.6 170.4 %all-gather.20.cloned.1.call-start = ((), (), s32[]{:S(2)}) async-start(), calls=%async_computation.14 | async-start | bytes 4325376 | tf_op jit(solution)/shard_map/all_gather | solution.py:124
  137.4 241.2 %all-gather.22.cloned.1.call-start = ((), (), s32[]{:S(2)}) async-start(), calls=%async_computation.15 | async-start | bytes 6488064 | tf_op jit(solution)/shard_map/all_gather | solution.py:179
  138.2 311.8 %all-gather.24.cloned.1.call-start = ((), (), s32[]{:S(2)}) async-start(), calls=%async_computation.16 | async-start | bytes 6488064 | tf_op jit(solution)/shard_map/all_gather | solution.py:180
  139.1 382.4 %all-gather.26.cloned.1.call-start = ((), (), s32[]{:S(2)}) async-start(), calls=%async_computation.17 | async-start | bytes 6488064 | tf_op jit(solution)/shard_map/all_gather | solution.py:181
  139.9 452.0 %reduce-scatter.12.cloned.1.call-start = ((), (), s32[]{:S(2)}) async-start(), calls=%async_computation.19 | async-start | bytes 2621440 | tf_op jit(solution)/shard_map/reduce_scatter | solution.py:243
  253.4 8.2 copy-start.3
  555.5 66.8 %reduce-scatter.10.cloned.1.call-start = ((), (), s32[]{:S(2)}) async-start(), calls=%async_computation.18 | async-start | bytes 2621440 | tf_op jit(solution)/shard_map/reduce_scatter | solution.py:240
  591.9 190.9 %reduce-scatter.18.cloned.1.call-start = ((), (), s32[]{:S(2)}) async-start(), calls=%async_computation.22 | async-start | bytes 4325376 | tf_op jit(solution)/shard_map/reduce_scatter | solution.py:280
  595.9 308.8 %reduce-scatter.16.cloned.1.call-start = ((), (), s32[]{:S(2)}) async-start(), calls=%async_computation.21 | async-start | bytes 4325376 | tf_op jit(solution)/shard_map/reduce_scatter | solution.py:279
  645.8 405.9 %reduce-scatter.14.cloned.1.call-start = ((), (), s32[]{:S(2)}) async-start(), calls=%async_computation.20 | async-start | bytes 8650752 | tf_op jit(solution)/shard_map/reduce_scatter | solution.py:278
  697.4 511.6 %reduce-scatter.22.cloned.1.call-start = ((), (), s32[]{:S(2)}) async-start(), calls=%async_computation.24 | async-start | bytes 12976128 | tf_op jit(solution)/shard_map/reduce_scatter | solution.py:205
  705.2 665.1 %reduce-scatter.24.cloned.1.call-start = ((), (), s32[]{:S(2)}) async-start(), calls=%async_computation.25 | async-start | bytes 12976128 | tf_op jit(solution)/shard_map/reduce_scatter | solution.py:206
  713.2 807.0 %reduce-scatter.20.cloned.1.call-start = ((), (), s32[]{:S(2)}) async-start(), calls=%async_computation.23 | async-start | bytes 8650752 | tf_op jit(solution)/shard_map/reduce_scatter | solution.py:281
  720.2 957.2 %reduce-scatter.26.cloned.1.call-start = ((), (), s32[]{:S(2)}) async-start(), calls=%async_computation.26 | async-start | bytes 12976128 | tf_op jit(solution)/shard_map/reduce_scatter | solution.py:207
  740.2 41.3 %copy-start.38 = (f32[256]{0:T(256)S(1)}, f32[256]{0:T(256)}, u32[]{:S(2)}) copy-start(f32[256]{0:T(256)} %get-tuple-element.49) | copy-start | bytes 3076
  (39 other events, 117.8 us)
Sparse Core Ops, SparseCore 0:
  11.5 59.0 all-gather.9
  74.0 55.2 all-gather.13
  131.4 21.4 all-gather.11
  156.2 62.0 all-gather.17
  220.2 21.3 all-gather.15
  244.9 62.0 all-gather.19
  310.5 68.0 all-gather.21
  382.0 68.0 all-gather.23
  453.5 67.9 all-gather.25
  555.7 29.9 reduce-scatter.11
  592.0 30.2 reduce-scatter.9
  624.5 141.1 reduce-scatter.17
  767.9 136.7 reduce-scatter.15
  906.9 144.7 reduce-scatter.13
  1057.6 151.3 reduce-scatter.21
  1215.8 154.4 reduce-scatter.23
  1372.5 147.7 reduce-scatter.19
  1526.1 151.2 reduce-scatter.25
where the time goes:
time: 1690 us
  waiting for transfers between devices  1300 us (77%)
  matrix products  189 us (11%)
  blocking collectives  81.7 us (5%)
  local copies, waits for them, and re-layouts  66.1 us (4%)
  other arithmetic  34.4 us (2%)
    reduce_scatter x1, waiting for transfers between devices, shards(): lax.psum_scatter(grad_up_full, ('dp', 'ctx'), scatter_dimension=0, tiled=...  160 us
    reduce_scatter x1, waiting for transfers between devices, shards(): lax.psum_scatter(grad_gate_full, ('dp', 'ctx'), scatter_dimension=0, tile...  156 us
    reduce_scatter x1, waiting for transfers between devices, shards(): lax.psum_scatter(grad_down_full, ('dp', 'ctx'), scatter_dimension=0, tile...  156 us
    reduce_scatter x1, waiting for transfers between devices, shards(): lax.psum_scatter(grad_out_full, ('dp', 'ctx'), scatter_dimension=0, tiled...  148 us
    reduce_scatter x1, waiting for transfers between devices, shards(): lax.psum_scatter(grad_query_full, ('dp', 'ctx'), scatter_dimension=0, til...  145 us
    reduce_scatter x1, waiting for transfers between devices, shards(): lax.psum_scatter(grad_key_full, ('dp', 'ctx'), scatter_dimension=0, tiled...  120 us
    unnamed x2, blocking collectives  81.7 us
    all_gather x1, waiting for transfers between devices, shards(): lax.all_gather(gate_local, ('dp', 'ctx'), axis=0, tiled=True)  66.3 us
  transfers between devices with their start and end apart: 18, of which 16 were waited for; matrix products, arithmetic and copies ran while one was open for 15% of the time, Pallas kernels for 0%

commit v1 on v0

v1 whole, which is shorter than its diff:
```python
import functools

import jax
import jax.numpy as jnp
from jax import lax
from jax.experimental import pallas as pl
from jax.experimental.pallas import tpu as pltpu
from jax.sharding import PartitionSpec as P

QUERY_HEADS = 16
KEY_VALUE_HEADS = 8
HEAD_SIZE = 128
FEEDFORWARD_UNITS = 3072
GROUPS = QUERY_HEADS // KEY_VALUE_HEADS
GROUP_WIDTH = (GROUPS + 2) * HEAD_SIZE

NORM_EPS = 1e-06
ROPE_THETA = 1000000.0
SCALE = HEAD_SIZE ** (-0.5)
BOTH = ("dp", "ctx")
bf16 = jnp.bfloat16
f32 = jnp.float32


def inv_rms(u):
    return lax.rsqrt(jnp.mean(u * u, axis=-1, keepdims=True) + NORM_EPS)


def norm_backward(u, r, gain, upstream):
    weighted = upstream * gain
    return r * weighted - u * r**3 * jnp.mean(weighted * u, axis=-1, keepdims=True)


def dot_nn(a, b):
    return lax.dot_general(a, b, (((1,), (0,)), ((), ())), preferred_element_type=f32)


def dot_tn(a, b):
    return lax.dot_general(a, b, (((0,), (0,)), ((), ())), preferred_element_type=f32)


def dot_nt(a, b):
    return lax.dot_general(a, b, (((1,), (1,)), ((), ())), preferred_element_type=f32)


def swap_halves(z):
    return pltpu.roll(z, HEAD_SIZE // 2, 1)


def rotate(z, cos, sin):
    return z * cos + swap_halves(z) * sin


def unrotate(g, cos, sin):
    return g * cos - swap_halves(g) * sin


def prepare(slot_ref, raw_ref, cos_ref, sin_ref, gains_ref, q_s, k_s, v_s):
    blocks = slot_ref.shape[0]
    size = raw_ref.shape[0] // blocks
    gain_q = gains_ref[0:1, :]
    gain_k = gains_ref[1:2, :]
    for b in range(blocks):
        src = pl.ds(pl.multiple_of(slot_ref[b] * size, size), size)
        dst = pl.ds(b * size, size)
        cos = cos_ref[src, :]
        sin = sin_ref[src, :]
        for g in range(GROUPS):
            z = raw_ref[src, g * HEAD_SIZE : (g + 1) * HEAD_SIZE]
            q_s[g, dst, :] = rotate(z * inv_rms(z) * gain_q, cos, sin).astype(bf16)
        z = raw_ref[src, GROUPS * HEAD_SIZE : (GROUPS + 1) * HEAD_SIZE]
        k_s[dst, :] = rotate(z * inv_rms(z) * gain_k, cos, sin).astype(bf16)
        v_s[dst, :] = raw_ref[src, (GROUPS + 1) * HEAD_SIZE :].astype(bf16)


def softmax_tile(q, k, start):
    scores = dot_nt(q, k) * SCALE
    rows = lax.broadcasted_iota(jnp.int32, scores.shape, 0) + start
    cols = lax.broadcasted_iota(jnp.int32, scores.shape, 1)
    scores = jnp.where(cols <= rows, scores, -1e30)
    expo = jnp.exp(scores - jnp.max(scores, axis=-1, keepdims=True))
    return expo / jnp.sum(expo, axis=-1, keepdims=True)


def forward_kernel(tile, slot_ref, raw_ref, cos_ref, sin_ref, gains_ref, o_ref, q_s, k_s, v_s, o_s):
    prepare(slot_ref, raw_ref, cos_ref, sin_ref, gains_ref, q_s, k_s, v_s)
    length = raw_ref.shape[0]
    for i in range(length // tile):
        end = (i + 1) * tile
        for g in range(GROUPS):
            p = softmax_tile(q_s[g, i * tile : end, :], k_s[:end, :], i * tile)
            o_s[i * tile : end, g * HEAD_SIZE : (g + 1) * HEAD_SIZE] = dot_nn(
                p.astype(bf16), v_s[:end, :]
            ).astype(bf16)
    blocks = slot_ref.shape[0]
    size = length // blocks
    for b in range(blocks):
        o_ref[pl.ds(pl.multiple_of(slot_ref[b] * size, size), size), :] = o_s[
            b * size : (b + 1) * size, :
        ]


def backward_kernel(
    tile, slot_ref, raw_ref, cos_ref, sin_ref, gains_ref, do_ref, d_ref, dg_ref,
    q_s, k_s, v_s, do_s, dq_s, dk_s, dv_s,
):
    prepare(slot_ref, raw_ref, cos_ref, sin_ref, gains_ref, q_s, k_s, v_s)
    length = raw_ref.shape[0]
    blocks = slot_ref.shape[0]
    size = length // blocks
    for b in range(blocks):
        do_s[b * size : (b + 1) * size, :] = do_ref[
            pl.ds(pl.multiple_of(slot_ref[b] * size, size), size), :
        ]
    dk_s[...] = jnp.zeros_like(dk_s)
    dv_s[...] = jnp.zeros_like(dv_s)
    for i in range(length // tile):
        end = (i + 1) * tile
        for g in range(GROUPS):
            q = q_s[g, i * tile : end, :]
            do = do_s[i * tile : end, g * HEAD_SIZE : (g + 1) * HEAD_SIZE]
            p = softmax_tile(q, k_s[:end, :], i * tile)
            dp = dot_nt(do, v_s[:end, :])
            delta = jnp.sum(p * dp, axis=-1, keepdims=True)
            ds = (p * (dp - delta) * SCALE).astype(bf16)
            dq_s[g, i * tile : end, :] = dot_nn(ds, k_s[:end, :])
            dk_s[:end, :] += dot_tn(ds, q)
            dv_s[:end, :] += dot_tn(p.astype(bf16), do)
    gain_q = gains_ref[0:1, :]
    gain_k = gains_ref[1:2, :]
    dgq = jnp.zeros((1, HEAD_SIZE), f32)
    dgk = jnp.zeros((1, HEAD_SIZE), f32)
    for b in range(blocks):
        src = pl.ds(pl.multiple_of(slot_ref[b] * size, size), size)
        dst = pl.ds(b * size, size)
        cos = cos_ref[src, :]
        sin = sin_ref[src, :]
        for g in range(GROUPS):
            cols = slice(g * HEAD_SIZE, (g + 1) * HEAD_SIZE)
            z = raw_ref[src, cols]
            r = inv_rms(z)
            grad = unrotate(dq_s[g, dst, :], cos, sin)
            dgq += jnp.sum(grad * z * r, axis=0, keepdims=True)
            d_ref[src, cols] = norm_backward(z, r, gain_q, grad).astype(bf16)
        cols = slice(GROUPS * HEAD_SIZE, (GROUPS + 1) * HEAD_SIZE)
        z = raw_ref[src, cols]
        r = inv_rms(z)
        grad = unrotate(dk_s[dst, :], cos, sin)
        dgk += jnp.sum(grad * z * r, axis=0, keepdims=True)
        d_ref[src, cols] = norm_backward(z, r, gain_k, grad).astype(bf16)
        d_ref[src, (GROUPS + 1) * HEAD_SIZE :] = dv_s[dst, :].astype(bf16)
    dg_ref[...] = jnp.concatenate([dgq, dgk, jnp.zeros((6, HEAD_SIZE), f32)], axis=0)[None]


def attention_specs(length):
    group = pl.BlockSpec((length, GROUP_WIDTH), lambda h, s: (0, h))
    heads = pl.BlockSpec((length, GROUPS * HEAD_SIZE), lambda h, s: (0, h))
    table = pl.BlockSpec((length, HEAD_SIZE), lambda h, s: (0, 0))
    gains = pl.BlockSpec((8, HEAD_SIZE), lambda h, s: (0, 0))
    return group, heads, table, gains


def attention_forward(slots, raw, cos, sin, gains):
    length = raw.shape[0]
    count = raw.shape[1] // GROUP_WIDTH
    group, heads, table, gain_spec = attention_specs(length)
    return pl.pallas_call(
        functools.partial(forward_kernel, 256),
        grid_spec=pltpu.PrefetchScalarGridSpec(
            num_scalar_prefetch=1,
            grid=(count,),
            in_specs=[group, table, table, gain_spec],
            out_specs=heads,
            scratch_shapes=[
                pltpu.VMEM((GROUPS, length, HEAD_SIZE), bf16),
                pltpu.VMEM((length, HEAD_SIZE), bf16),
                pltpu.VMEM((length, HEAD_SIZE), bf16),
                pltpu.VMEM((length, GROUPS * HEAD_SIZE), bf16),
            ],
        ),
        out_shape=jax.ShapeDtypeStruct((length, count * GROUPS * HEAD_SIZE), bf16),
        compiler_params=pltpu.CompilerParams(vmem_limit_bytes=40 * 2**20),
        cost_estimate=pl.CostEstimate(
            flops=count * GROUPS * 4 * length * length * HEAD_SIZE,
            bytes_accessed=length * count * GROUP_WIDTH * 4,
            transcendentals=count * GROUPS * length * length,
        ),
    )(slots, raw, cos, sin, gains)


def attention_backward(slots, raw, cos, sin, gains, grad_o):
    length = raw.shape[0]
    count = raw.shape[1] // GROUP_WIDTH
    group, heads, table, gain_spec = attention_specs(length)
    return pl.pallas_call(
        functools.partial(backward_kernel, 256),
        grid_spec=pltpu.PrefetchScalarGridSpec(
            num_scalar_prefetch=1,
            grid=(count,),
            in_specs=[group, table, table, gain_spec, heads],
            out_specs=[group, pl.BlockSpec((1, 8, HEAD_SIZE), lambda h, s: (h, 0, 0))],
            scratch_shapes=[
                pltpu.VMEM((GROUPS, length, HEAD_SIZE), bf16),
                pltpu.VMEM((length, HEAD_SIZE), bf16),
                pltpu.VMEM((length, HEAD_SIZE), bf16),
                pltpu.VMEM((length, GROUPS * HEAD_SIZE), bf16),
                pltpu.VMEM((GROUPS, length, HEAD_SIZE), f32),
                pltpu.VMEM((length, HEAD_SIZE), f32),
                pltpu.VMEM((length, HEAD_SIZE), f32),
            ],
        ),
        out_shape=[
            jax.ShapeDtypeStruct((length, count * GROUP_WIDTH), bf16),
            jax.ShapeDtypeStruct((count, 8, HEAD_SIZE), f32),
        ],
        compiler_params=pltpu.CompilerParams(vmem_limit_bytes=40 * 2**20),
        cost_estimate=pl.CostEstimate(
            flops=count * GROUPS * 10 * length * length * HEAD_SIZE,
            bytes_accessed=length * count * GROUP_WIDTH * 6,
            transcendentals=count * GROUPS * length * length,
        ),
    )(slots, raw, cos, sin, gains, grad_o)


def gather_rows(x, axis):
    return lax.all_gather(x, axis, axis=0, tiled=True)


def sum_rows(x, axis):
    return lax.psum_scatter(x.astype(bf16), axis, scatter_dimension=0, tiled=True)


def shards(
    hidden_in,
    cotangent,
    block_order,
    w_query,
    key_weight,
    value_weight,
    w_out,
    w_gate,
    w_up,
    w_down,
    norm_gains,
):
    width = hidden_in.shape[1]
    dp, ctx = lax.axis_size("dp"), lax.axis_size("ctx")
    devices = dp * ctx
    length = hidden_in.shape[0] * ctx
    units = FEEDFORWARD_UNITS // ctx
    kv_local = KEY_VALUE_HEADS // ctx
    qkv_width = kv_local * GROUP_WIDTH
    heads_width = kv_local * GROUPS * HEAD_SIZE

    orders = block_order[0]
    blocks = orders.shape[0]
    size = length // blocks
    slots = jnp.sum(
        jnp.where(
            orders[None, :] == jnp.arange(blocks, dtype=jnp.int32)[:, None],
            jnp.arange(blocks, dtype=jnp.int32)[None, :],
            0,
        ),
        axis=1,
    ).astype(jnp.int32)
    places = (orders[:, None] * size + jnp.arange(size, dtype=jnp.int32)[None, :]).reshape(-1)
    half = HEAD_SIZE // 2
    inverse = ROPE_THETA ** (-(jnp.arange(half, dtype=f32) * 2.0 / HEAD_SIZE))
    angles = places.astype(f32)[:, None] * inverse[None, :]
    cos, sin = jnp.cos(angles), jnp.sin(angles)
    cos_table = jnp.concatenate([cos, cos], axis=1)
    sin_table = jnp.concatenate([-sin, sin], axis=1)

    x_all = gather_rows(hidden_in, "ctx")
    gain_piece = norm_gains.shape[0]
    gains_all = gather_rows(
        jnp.pad(norm_gains[None, :], ((0, 15), (0, 128 - gain_piece))), BOTH
    )
    gains = gains_all.reshape(devices, 16, 128)[:, 0, :gain_piece].reshape(-1).astype(f32)
    gain_one = gains[:width]
    gain_two = gains[width : 2 * width]
    head_gains = jnp.pad(gains[2 * width :].reshape(2, HEAD_SIZE), ((0, 6), (0, 0)))

    rows = w_query.shape[0] // (QUERY_HEADS * HEAD_SIZE)
    qkv_rows = jnp.concatenate(
        [
            w_query.reshape(rows, KEY_VALUE_HEADS, GROUPS * HEAD_SIZE),
            key_weight.reshape(rows, KEY_VALUE_HEADS, HEAD_SIZE),
            value_weight.reshape(rows, KEY_VALUE_HEADS, HEAD_SIZE),
        ],
        axis=2,
    ).reshape(rows, ctx, qkv_width)
    mlp_rows = jnp.concatenate(
        [w_gate.reshape(rows, ctx, units), w_up.reshape(rows, ctx, units)], axis=2
    )
    column_rows = jnp.concatenate([qkv_rows, mlp_rows], axis=2).transpose(1, 0, 2)
    column_rows = lax.all_to_all(column_rows, "ctx", 0, 0, tiled=True)
    column_rows = column_rows.reshape(ctx * rows, -1)
    row_parts = jnp.concatenate([w_out.reshape(-1, width), w_down.reshape(-1, width)], axis=0)
    out_rows = w_out.shape[0] // width
    there = [(d, (d % dp) * ctx + d // dp) for d in range(devices)]
    back = [(b, a) for a, b in there]
    row_parts = lax.ppermute(row_parts, BOTH, there)

    qkv_w = gather_rows(column_rows[:, :qkv_width], "dp")
    out_w = gather_rows(row_parts[:out_rows], "dp")
    mlp_w = gather_rows(column_rows[:, qkv_width:], "dp")
    down_w = gather_rows(row_parts[out_rows:], "dp")
    dy_all = gather_rows(cotangent, "ctx")

    x_full = x_all.astype(f32)
    a_all = (x_full * inv_rms(x_full) * gain_one).astype(bf16)
    raw = dot_nn(a_all, qkv_w)
    o_all = attention_forward(slots, raw, cos_table, sin_table, head_gains)
    x = hidden_in.astype(f32)
    scale_one = inv_rms(x)
    middle = x + sum_rows(dot_nn(o_all, out_w), "ctx").astype(f32)
    scale_two = inv_rms(middle)
    b_all = gather_rows((middle * scale_two * gain_two).astype(bf16), "ctx")

    both = dot_nn(b_all, mlp_w)
    gate, up = both[:, :units], both[:, units:]
    sigmoid = jax.nn.sigmoid(gate)
    activated = gate * sigmoid
    hidden = (activated * up).astype(bf16)
    grad_hidden = dot_nt(dy_all, down_w)
    grad_both = jnp.concatenate(
        [
            (grad_hidden * up * sigmoid * (1.0 + gate * (1.0 - sigmoid))).astype(bf16),
            (grad_hidden * activated).astype(bf16),
        ],
        axis=1,
    )
    grad_b = sum_rows(dot_nt(grad_both, mlp_w), "ctx").astype(f32)
    block_out = (middle + sum_rows(dot_nn(hidden, down_w), "ctx").astype(f32)).astype(bf16)
    grad_mlp = sum_rows(dot_tn(b_all, grad_both), "dp")
    grad_down = sum_rows(dot_tn(hidden, dy_all), "dp")

    grad_gain_two = jnp.sum(grad_b * middle * scale_two, axis=0)
    grad_middle = cotangent.astype(f32) + norm_backward(middle, scale_two, gain_two, grad_b)
    dom_all = gather_rows(grad_middle.astype(bf16), "ctx")
    grad_o = dot_nt(dom_all, out_w).astype(bf16)
    grad_out = sum_rows(dot_tn(o_all, dom_all), "dp")
    grad_raw, grad_head_gains = attention_backward(
        slots, raw, cos_table, sin_table, head_gains, grad_o
    )
    grad_a = sum_rows(dot_nt(grad_raw, qkv_w), "ctx").astype(f32)
    grad_qkv = sum_rows(dot_tn(a_all, grad_raw), "dp")
    grad_gain_one = jnp.sum(grad_a * x * scale_one, axis=0)
    grad_in = grad_middle + norm_backward(x, scale_one, gain_one, grad_a)

    grad_gains = jnp.concatenate(
        [grad_gain_one, grad_gain_two, jnp.sum(grad_head_gains, axis=0)[:2].reshape(-1)]
    ).reshape(devices, 1, gain_piece)
    grad_gains = jnp.pad(grad_gains, ((0, 0), (0, 7), (0, 128 - gain_piece)))
    grad_gains = lax.psum_scatter(
        grad_gains.reshape(devices * 8, 128), BOTH, scatter_dimension=0, tiled=True
    )[0, :gain_piece]

    columns = jnp.concatenate([grad_qkv, grad_mlp], axis=1).reshape(ctx, rows, -1)
    columns = lax.all_to_all(columns, "ctx", 0, 0, tiled=True).transpose(1, 0, 2).astype(f32)
    own_qkv = columns[:, :, :qkv_width].reshape(rows, KEY_VALUE_HEADS, GROUP_WIDTH)
    own_mlp = columns[:, :, qkv_width:]
    row_grads = lax.ppermute(jnp.concatenate([grad_out, grad_down], axis=0), BOTH, back)
    row_grads = row_grads.astype(f32)
    split = GROUPS * HEAD_SIZE
    return (
        block_out,
        grad_in,
        own_qkv[:, :, :split].reshape(-1),
        own_qkv[:, :, split : split + HEAD_SIZE].reshape(-1),
        own_qkv[:, :, split + HEAD_SIZE :].reshape(-1),
        row_grads[:out_rows].reshape(-1),
        own_mlp[:, :, :units].reshape(-1),
        own_mlp[:, :, units:].reshape(-1),
        row_grads[out_rows:].reshape(-1),
        grad_gains,
    )


def solution(mesh):
    rows = P(("dp", "ctx"), None)
    flat = P(("dp", "ctx"))
    return jax.shard_map(
        shards,
        mesh=mesh,
        in_specs=(rows, rows, P("dp", None)) + (flat,) * 8,
        out_specs=(rows, rows) + (flat,) * 8,
        check_vma=False,
    )
```

time: 1690 us -> 912 us (0.54)
  waiting for transfers between devices: 1300 us -> 668 us
  matrix products: 189 us -> 62.8 us
  local copies, waits for them, and re-layouts: 66.1 us -> 23.2 us
  Pallas kernels: 0 us -> 35.5 us
    reduce_scatter x9 -> x8, waiting for transfers between devices: 909 us -> 342 us  [sum_rows(): lax.psum_scatter(x.astype(bf16), axis, scatter_dimension=0, tiled=True)]
    all_gather x9 -> x8, waiting for transfers between devices: 389 us -> 199 us  [gather_rows(): return lax.all_gather(x, axis, axis=0, tiled=True)]
    dot_general x27 -> x12, matrix products: 189 us -> 62.8 us  [the longest x4 21.6 us: dot_nn(): lax.dot_general(a, b, (((1,), (0,)), ((), ())), preferred_element_type=f32)]
    unnamed x18, waiting for transfers between devices: 0.29 us -> 127 us
    unnamed x2 -> x0, blocking collectives: 81.7 us -> none
    all_gather x0 -> x1, blocking collectives: none -> 52.9 us  [gather_rows(): return lax.all_gather(x, axis, axis=0, tiled=True)]
    pallas_call x0 -> x2, Pallas kernels: none -> 35.5 us  [the longest x1 23.3 us: attention_backward(): pl.pallas_call(functools.partial(backward_kernel, 256), grid_spec=pltpu.P...]
    unnamed x107 -> x50, local copies, waits for them, and re-layouts: 36.6 us -> 12.7 us
  transfers between devices with their start and end apart: 18 -> 20, of which waited for: 16 -> 16; matrix products, arithmetic and copies ran while one was open for 15% -> 8% of each run, Pallas kernels for 0% -> 4%
where the time goes in v1:
time: 912 us; the launch traced here: 902 us
  waiting for transfers between devices  668 us (73%)
  blocking collectives  71.2 us (8%)
  matrix products  62.8 us (7%)
  Pallas kernels  35.5 us (4%)
  local copies, waits for them, and re-layouts  23.2 us (3%)
  other arithmetic  20.7 us (2%)
  between operations  14.9 us (2%)
    reduce_scatter x8, waiting for transfers between devices, sum_rows(): lax.psum_scatter(x.astype(bf16), axis, scatter_dimension=0, tiled=True)  342 us
    all_gather x8, waiting for transfers between devices, gather_rows(): return lax.all_gather(x, axis, axis=0, tiled=True)  199 us
    unnamed x18, waiting for transfers between devices  127 us
    all_gather x1, blocking collectives, gather_rows(): return lax.all_gather(x, axis, axis=0, tiled=True)  52.9 us
    pallas_call x1, Pallas kernels, attention_backward(): pl.pallas_call(functools.partial(backward_kernel, 256), grid_spec=pltpu.P...  23.3 us
    dot_general x4, matrix products, dot_nn(): lax.dot_general(a, b, (((1,), (0,)), ((), ())), preferred_element_type=f32)  21.6 us
    dot_general x4, matrix products, dot_tn(): lax.dot_general(a, b, (((0,), (0,)), ((), ())), preferred_element_type=f32)  21.5 us
    dot_general x4, matrix products, dot_nt(): lax.dot_general(a, b, (((1,), (1,)), ((), ())), preferred_element_type=f32)  19.7 us
  transfers between devices with their start and end apart: 20, of which 16 were waited for; matrix products, arithmetic and copies ran while one was open for 8% of the time, Pallas kernels for 4%

profile of v1, /device:TPU:0, one launch (start us, length us, event | category | flops | bytes accessed | tf_op | source)
XLA Modules:
  0.0 901.9 jit_solution(7543697208591265099)
XLA Ops:
  11.6 18.3 %all_to_all.10 = bf16[4,32,2560]{2,1,0:T(8,128)(2,1)S(1)} all-to-all(bf16[4,32,2560]{2,1,0:T(8,128)(2,1)S(1)} %copy.37), channel_id=1, replica_groups=mesh['dp'=8,'ctx'=4] {'ctx'}, dimensions={0} | all-to-all | bytes 1310720 | tf_op jit(solution)/shard_map/all_to_all | solution.py:297
  31.6 52.9 %all_gather.28 = bf16[512,128]{1,0:T(8,128)(2,1)S(1)} all-gather(bf16[16,128]{1,0:T(8,128)(2,1)S(1)} %pad.14), channel_id=1, replica_groups=mesh['dp'=8,'ctx'=4] {'dp','ctx'}, dimensions={0}, use_global_device_ids=true | all-gather | bytes 135168 | tf_op jit(solution)/shard_map/all_gather | solution.py:226
  90.1 15.2 %all-gather.11.cloned.1.call-done = bf16[1024,1024]{1,0:T(8,128)(2,1)} async-done(((bf16[128,1024]{1,0:T(8,128)(2,1)}), bf16[1024,1024]{1,0:T(8,128)(2,1)}) %all-gather.11.cloned.1.call-update) | async-done | bytes 2097168 | tf_op jit(solution)/shard_map/all_gather | solution.py:226
  109.9 12.2 %shard_map.186 = bf16[1024,512]{1,0:T(8,128)(2,1)S(1)} custom-call(s32[8]{0:T(128)S(1)} %select_reduce_fusion.slot_ref, f32[1024,1024]{1,0:T(8,128)S(1)} %fusion.26.raw_ref, f32[1024,128]{1,0:T(8,128)S(1)} %get-tuple-element.37.cos_ref, f32[1024,128]{1,0:T(8,128)S(1)} %get-tuple-element.38.sin_ref, f32[8,128]{1,0:T(8,128)S(1)} %pad_convert_fusion.gains_ref), custom_call_target="tpu_custom_call" | custom-call | flops 2147483648 | bytes 4194304 | tf_op jit(solution)/shard_map/pallas_call | solution.py:167
  124.2 22.6 %all-gather.13.cloned.1.call-done = bf16[512,1024]{1,0:T(8,128)(2,1)} async-done(((bf16[64,1024]{1,0:T(8,128)(2,1)}), bf16[512,1024]{1,0:T(8,128)(2,1)}) %all-gather.13.cloned.1.call-update) | async-done | bytes 1048592 | tf_op jit(solution)/shard_map/all_gather | solution.py:226
  151.5 29.4 %reduce-scatter.9.cloned.1.call-done = bf16[256,1024]{1,0:T(8,128)(2,1)} async-done(((bf16[1024,1024]{1,0:T(8,128)(2,1)}), bf16[256,1024]{1,0:T(8,128)(2,1)}) %reduce-scatter.9.cloned.1.call-update) | async-done | bytes 524304 | tf_op jit(solution)/shard_map/reduce_scatter | solution.py:230
  186.1 58.2 %all-gather.17.cloned.1.call-done = bf16[1024,1536]{1,0:T(8,128)(2,1)} async-done(((bf16[128,1536]{1,0:T(8,128)(2,1)}), bf16[1024,1536]{1,0:T(8,128)(2,1)}) %all-gather.17.cloned.1.call-update) | async-done | bytes 3145744 | tf_op jit(solution)/shard_map/all_gather | solution.py:226
  244.3 23.3 %all-gather.15.cloned.1.call-done = bf16[1024,1024]{1,0:T(8,128)(2,1)} async-done(((bf16[256,1024]{1,0:T(8,128)(2,1)}), bf16[1024,1024]{1,0:T(8,128)(2,1)}) %all-gather.15.cloned.1.call-update) | async-done | bytes 2097168 | tf_op jit(solution)/shard_map/all_gather | solution.py:226
  267.6 8.6 fusion.34
  276.2 38.7 %all-gather.19.cloned.1.call-done = bf16[768,1024]{1,0:T(8,128)(2,1)} async-done(((bf16[96,1024]{1,0:T(8,128)(2,1)}), bf16[768,1024]{1,0:T(8,128)(2,1)}) %all-gather.19.cloned.1.call-update) | async-done | bytes 1572880 | tf_op jit(solution)/shard_map/all_gather | solution.py:226
  314.8 23.1 %all-gather.21.cloned.1.call-done = bf16[1024,1024]{1,0:T(8,128)(2,1)} async-done(((bf16[256,1024]{1,0:T(8,128)(2,1)}), bf16[1024,1024]{1,0:T(8,128)(2,1)}) %all-gather.21.cloned.1.call-update) | async-done | bytes 2097168 | tf_op jit(solution)/shard_map/all_gather | solution.py:226
  337.9 8.1 fusion.5
  352.4 31.5 %reduce-scatter.13.cloned.1.call-done = bf16[256,1024]{1,0:T(8,128)(2,1)} async-done(((bf16[1024,1024]{1,0:T(8,128)(2,1)}), bf16[256,1024]{1,0:T(8,128)(2,1)}) %reduce-scatter.13.cloned.1.call-update) | async-done | bytes 524304 | tf_op jit(solution)/shard_map/reduce_scatter | solution.py:230
  393.1 17.5 %all-gather.23.cloned.1.call-done = bf16[1024,1024]{1,0:T(8,128)(2,1)} async-done(((bf16[256,1024]{1,0:T(8,128)(2,1)}), bf16[1024,1024]{1,0:T(8,128)(2,1)}) %all-gather.23.cloned.1.call-update) | async-done | bytes 2097168 | tf_op jit(solution)/shard_map/all_gather | solution.py:226
  417.9 23.3 %shard_map.187 = (bf16[1024,1024]{1,0:T(8,128)(2,1)S(1)}, f32[2,8,128]{2,1,0:T(8,128)S(1)}) custom-call(s32[8]{0:T(128)S(1)} %select_reduce_fusion.slot_ref, f32[1024,1024]{1,0:T(8,128)S(1)} %copy-done.1, f32[1024,128]{1,0:T(8,128)S(1)} %get-tuple-element.37.cos_ref, f32[1024,128]{1,0:T(8,128)S(1)} %get-tuple-element.38.sin_ref, ...), custom_call_target="tpu_custom_call" | custom-call | flops 5368709120 | bytes 6291456 | tf_op jit(solution)/shard_map/pallas_call | solution.py:195
  447.9 7.0 convolution_convert_fusion
  456.5 5.6 convolution_convert_fusion.1
  468.0 11.0 %reduce-scatter.23.cloned.1.call-done = bf16[96,1024]{1,0:T(8,128)(2,1)} async-done(((bf16[768,1024]{1,0:T(8,128)(2,1)}), bf16[96,1024]{1,0:T(8,128)(2,1)}) %reduce-scatter.23.cloned.1.call-update) | async-done | bytes 196624 | tf_op jit(solution)/shard_map/reduce_scatter | solution.py:230
  479.0 66.6 %reduce-scatter.21.cloned.1.call-done = bf16[64,1024]{1,0:T(8,128)(2,1)} async-done(((bf16[512,1024]{1,0:T(8,128)(2,1)}), bf16[64,1024]{1,0:T(8,128)(2,1)}) %reduce-scatter.21.cloned.1.call-update) | async-done | bytes 131088 | tf_op jit(solution)/shard_map/reduce_scatter | solution.py:230
  549.1 29.5 %reduce-scatter.15.cloned.1.call-done = bf16[256,1024]{1,0:T(8,128)(2,1)} async-done(((bf16[1024,1024]{1,0:T(8,128)(2,1)}), bf16[256,1024]{1,0:T(8,128)(2,1)}) %reduce-scatter.15.cloned.1.call-update) | async-done | bytes 524304 | tf_op jit(solution)/shard_map/reduce_scatter | solution.py:230
  580.1 76.8 %reduce-scatter.19.cloned.1.call-done = bf16[128,1536]{1,0:T(8,128)(2,1)} async-done(((bf16[1024,1536]{1,0:T(8,128)(2,1)}), bf16[128,1536]{1,0:T(8,128)(2,1)}) %reduce-scatter.19.cloned.1.call-update) | async-done | bytes 393232 | tf_op jit(solution)/shard_map/reduce_scatter | solution.py:230
  656.9 70.6 %reduce-scatter.17.cloned.1.call-done = bf16[128,1024]{1,0:T(8,128)(2,1)} async-done(((bf16[1024,1024]{1,0:T(8,128)(2,1)}), bf16[128,1024]{1,0:T(8,128)(2,1)}) %reduce-scatter.17.cloned.1.call-update) | async-done | bytes 262160 | tf_op jit(solution)/shard_map/reduce_scatter | solution.py:230
  733.7 26.9 %reduce-scatter.11.cloned.1.call-done = bf16[256,1024]{1,0:T(8,128)(2,1)} async-done(((bf16[1024,1024]{1,0:T(8,128)(2,1)}), bf16[256,1024]{1,0:T(8,128)(2,1)}) %reduce-scatter.11.cloned.1.call-update) | async-done | bytes 524304 | tf_op jit(solution)/shard_map/reduce_scatter | solution.py:230
  763.7 125.4 %all-reduce.6.cloned.1.call-done = f32[256,128]{1,0:T(8,128)} async-done(((f32[256,128]{1,0:T(8,128)}), f32[256,128]{1,0:T(8,128)}) %all-reduce.6.cloned.1.call-update) | async-done | bytes 131088
  (157 shorter events, 84.8 us)
Async XLA Ops:
  7.2 80.9 %all-gather.9.cloned.1.call-start = ((), (), s32[]{:S(2)}) async-start(), calls=%async_computation.10 | async-start | bytes 2621440 | tf_op jit(solution)/shard_map/all_gather | solution.py:226
  7.9 97.4 %all-gather.11.cloned.1.call-start = ((), (), s32[]{:S(2)}) async-start(), calls=%async_computation.11 | async-start | bytes 2359296 | tf_op jit(solution)/shard_map/all_gather | solution.py:226
  11.5 73.2 %copy-start.18 = (s32[1,8]{1,0:T(1,128)S(1)}, s32[1,8]{1,0:T(1,128)}, u32[]{:S(2)}) copy-start(s32[1,8]{1,0:T(1,128)} %param.13) | copy-start | bytes 100
  30.6 116.2 %all-gather.13.cloned.1.call-start = ((), (), s32[]{:S(2)}) async-start(), calls=%async_computation.12 | async-start | bytes 1179648 | tf_op jit(solution)/shard_map/all_gather | solution.py:226
  30.9 54.1 %collective-permute-start = (bf16[160,1024]{1,0:T(8,128)(2,1)S(1)}, bf16[160,1024]{1,0:T(8,128)(2,1)S(1)}, u32[]{:S(2)}, u32[]{:S(2)}) collective-permute-start(bf16[160,1024]{1,0:T(8,128)(2,1)S(1)} %pad_maximum_fusion.8), channel_id=1, source_target_pairs={{0,0},{1,4},{2,8},{3,12},{4,16},{5,20},{6,24},{7,28},{8,1},{9,5},{... | collective-permute-start | bytes 983048 | tf_op jit(solution)/shard_map/ppermute | solution.py:303
  85.7 95.2 %reduce-scatter.9.cloned.1.call-start = ((), (), s32[]{:S(2)}) async-start(), calls=%async_computation.13 | async-start | bytes 2621440 | tf_op jit(solution)/shard_map/reduce_scatter | solution.py:230
  150.6 93.7 %all-gather.17.cloned.1.call-start = ((), (), s32[]{:S(2)}) async-start(), calls=%async_computation.15 | async-start | bytes 3538944 | tf_op jit(solution)/shard_map/all_gather | solution.py:226
  151.5 33.0 %copy-start.9 = (bf16[160,1024]{1,0:T(8,128)(2,1)S(1)}, bf16[160,1024]{1,0:T(8,128)(2,1)}, u32[]{:S(2)}) copy-start(bf16[160,1024]{1,0:T(8,128)(2,1)} %copy-done.8) | copy-start | bytes 983044
  151.5 116.1 %all-gather.15.cloned.1.call-start = ((), (), s32[]{:S(2)}) async-start(), calls=%async_computation.14 | async-start | bytes 2621440 | tf_op jit(solution)/shard_map/all_gather | solution.py:226
  184.4 130.5 %all-gather.19.cloned.1.call-start = ((), (), s32[]{:S(2)}) async-start(), calls=%async_computation.16 | async-start | bytes 1769472 | tf_op jit(solution)/shard_map/all_gather | solution.py:226
  185.1 152.7 %all-gather.21.cloned.1.call-start = ((), (), s32[]{:S(2)}) async-start(), calls=%async_computation.18 | async-start | bytes 2621440 | tf_op jit(solution)/shard_map/all_gather | solution.py:226
  185.9 198.0 %reduce-scatter.13.cloned.1.call-start = ((), (), s32[]{:S(2)}) async-start(), calls=%async_computation.19 | async-start | bytes 2621440 | tf_op jit(solution)/shard_map/reduce_scatter | solution.py:230
  352.3 58.4 %all-gather.23.cloned.1.call-start = ((), (), s32[]{:S(2)}) async-start(), calls=%async_computation.20 | async-start | bytes 2621440 | tf_op jit(solution)/shard_map/all_gather | solution.py:226
  387.9 91.1 %reduce-scatter.23.cloned.1.call-start = ((), (), s32[]{:S(2)}) async-start(), calls=%async_computation.25 | async-start | bytes 1769472 | tf_op jit(solution)/shard_map/reduce_scatter | solution.py:230
  393.1 152.5 %reduce-scatter.21.cloned.1.call-start = ((), (), s32[]{:S(2)}) async-start(), calls=%async_computation.24 | async-start | bytes 1179648 | tf_op jit(solution)/shard_map/reduce_scatter | solution.py:230
  414.5 164.1 %reduce-scatter.15.cloned.1.call-start = ((), (), s32[]{:S(2)}) async-start(), calls=%async_computation.21 | async-start | bytes 2621440 | tf_op jit(solution)/shard_map/reduce_scatter | solution.py:230
  446.3 210.6 %reduce-scatter.19.cloned.1.call-start = ((), (), s32[]{:S(2)}) async-start(), calls=%async_computation.23 | async-start | bytes 3538944 | tf_op jit(solution)/shard_map/reduce_scatter | solution.py:230
  454.9 272.7 %reduce-scatter.17.cloned.1.call-start = ((), (), s32[]{:S(2)}) async-start(), calls=%async_computation.22 | async-start | bytes 2359296 | tf_op jit(solution)/shard_map/reduce_scatter | solution.py:230
  462.1 298.6 %reduce-scatter.11.cloned.1.call-start = ((), (), s32[]{:S(2)}) async-start(), calls=%async_computation.17 | async-start | bytes 2621440 | tf_op jit(solution)/shard_map/reduce_scatter | solution.py:230
  546.7 0.7 collective-permute-start.1
  549.1 211.6 %copy-start.6 = (bf16[256,1024]{1,0:T(8,128)(2,1)S(1)}, bf16[256,1024]{1,0:T(8,128)(2,1)}, u32[]{:S(2)}) copy-start(bf16[256,1024]{1,0:T(8,128)(2,1)} %param.12) | copy-start | bytes 1572868
  549.1 211.6 %copy-start.7 = (bf16[256,1024]{1,0:T(8,128)(2,1)S(1)}, bf16[256,1024]{1,0:T(8,128)(2,1)}, u32[]{:S(2)}) copy-start(bf16[256,1024]{1,0:T(8,128)(2,1)} %reduce-scatter.13.cloned.1.call-done) | copy-start | bytes 1572868
  729.5 160.7 %all-to-all-start.1 = ((bf16[4,32,2560]{2,1,0:T(8,128)(2,1)}), bf16[4,32,2560]{2,1,0:T(8,128)(2,1)S(1)}, u32[]{:S(2)}, u32[]{:S(2)}) async-start(bf16[4,32,2560]{2,1,0:T(8,128)(2,1)} %bitcast.9), calls=%async_computation.7 | async-start | bytes 1310720 | tf_op jit(solution)/shard_map/all_to_all | solution.py:361
  733.0 156.1 %all-reduce.6.cloned.1.call-start = ((), (), s32[]{:S(2)}) async-start(), calls=%async_computation.26 | async-start | bytes 262144
  (17 other events, 174.3 us)
Sparse Core Ops, SparseCore 0:
  9.6 28.9 all-gather.8
  41.3 64.0 all-gather.10
  108.0 38.6 all-gather.12
  150.8 30.1 reduce-scatter.8
  183.8 60.4 all-gather.16
  246.4 21.1 all-gather.14
  270.6 44.1 all-gather.18
  316.5 21.3 all-gather.20
  352.4 31.4 reduce-scatter.12
  388.1 22.5 all-gather.22
  414.1 64.8 reduce-scatter.22
  483.2 62.3 reduce-scatter.20
  548.2 30.4 reduce-scatter.14
  582.5 74.4 reduce-scatter.18
  660.7 66.7 reduce-scatter.16
  730.1 30.5 reduce-scatter.10
  766.6 122.3 all-reduce.5

commit v2 on v1

--- a/solution.py
+++ b/solution.py
@@ -271,7 +271,8 @@
     cos_table = jnp.concatenate([cos, cos], axis=1)
     sin_table = jnp.concatenate([-sin, sin], axis=1)
 
-    x_all = gather_rows(hidden_in, "ctx")
+    both_all = gather_rows(jnp.concatenate([hidden_in, cotangent], axis=1), "ctx")
+    x_all, dy_all = both_all[:, :width], both_all[:, width:]
     gain_piece = norm_gains.shape[0]
     gains_all = gather_rows(
         jnp.pad(norm_gains[None, :], ((0, 15), (0, 128 - gain_piece))), BOTH
@@ -302,11 +303,11 @@
     back = [(b, a) for a, b in there]
     row_parts = lax.ppermute(row_parts, BOTH, there)
 
-    qkv_w = gather_rows(column_rows[:, :qkv_width], "dp")
-    out_w = gather_rows(row_parts[:out_rows], "dp")
-    mlp_w = gather_rows(column_rows[:, qkv_width:], "dp")
-    down_w = gather_rows(row_parts[out_rows:], "dp")
-    dy_all = gather_rows(cotangent, "ctx")
+    column_w = gather_rows(column_rows, "dp")
+    qkv_w, mlp_w = column_w[:, :qkv_width], column_w[:, qkv_width:]
+    row_w = gather_rows(row_parts, "dp").reshape(dp, -1, width)
+    out_w = row_w[:, :out_rows].reshape(-1, width)
+    down_w = row_w[:, out_rows:].reshape(-1, width)
 
     x_full = x_all.astype(f32)
     a_all = (x_full * inv_rms(x_full) * gain_one).astype(bf16)
@@ -331,37 +332,50 @@
         ],
         axis=1,
     )
-    grad_b = sum_rows(dot_nt(grad_both, mlp_w), "ctx").astype(f32)
-    block_out = (middle + sum_rows(dot_nn(hidden, down_w), "ctx").astype(f32)).astype(bf16)
-    grad_mlp = sum_rows(dot_tn(b_all, grad_both), "dp")
-    grad_down = sum_rows(dot_tn(hidden, dy_all), "dp")
+    sums = sum_rows(
+        jnp.concatenate(
+            [dot_nt(grad_both, mlp_w).astype(bf16), dot_nn(hidden, down_w).astype(bf16)], axis=1
+        ),
+        "ctx",
+    ).astype(f32)
+    grad_b = sums[:, :width]
+    block_out = (middle + sums[:, width:]).astype(bf16)
+    grad_mlp = dot_tn(b_all, grad_both).astype(bf16)
+    grad_down = dot_tn(hidden, dy_all).astype(bf16)
 
     grad_gain_two = jnp.sum(grad_b * middle * scale_two, axis=0)
     grad_middle = cotangent.astype(f32) + norm_backward(middle, scale_two, gain_two, grad_b)
     dom_all = gather_rows(grad_middle.astype(bf16), "ctx")
     grad_o = dot_nt(dom_all, out_w).astype(bf16)
-    grad_out = sum_rows(dot_tn(o_all, dom_all), "dp")
+    grad_out = dot_tn(o_all, dom_all).astype(bf16)
+    row_grads = jnp.concatenate(
+        [grad_out.reshape(dp, -1, width), grad_down.reshape(dp, -1, width)], axis=1
+    )
+    row_grads = sum_rows(row_grads.reshape(-1, width), "dp")
     grad_raw, grad_head_gains = attention_backward(
         slots, raw, cos_table, sin_table, head_gains, grad_o
     )
     grad_a = sum_rows(dot_nt(grad_raw, qkv_w), "ctx").astype(f32)
-    grad_qkv = sum_rows(dot_tn(a_all, grad_raw), "dp")
+    grad_qkv = dot_tn(a_all, grad_raw).astype(bf16)
     grad_gain_one = jnp.sum(grad_a * x * scale_one, axis=0)
     grad_in = grad_middle + norm_backward(x, scale_one, gain_one, grad_a)
 
     grad_gains = jnp.concatenate(
         [grad_gain_one, grad_gain_two, jnp.sum(grad_head_gains, axis=0)[:2].reshape(-1)]
-    ).reshape(devices, 1, gain_piece)
-    grad_gains = jnp.pad(grad_gains, ((0, 0), (0, 7), (0, 128 - gain_piece)))
-    grad_gains = lax.psum_scatter(
-        grad_gains.reshape(devices * 8, 128), BOTH, scatter_dimension=0, tiled=True
-    )[0, :gain_piece]
-
-    columns = jnp.concatenate([grad_qkv, grad_mlp], axis=1).reshape(ctx, rows, -1)
+    )
+    lines = grad_gains.shape[0] // 128
+    grad_gains = jnp.pad(grad_gains.reshape(lines, 128), ((0, -lines % 8), (0, 0)))
+    grad_gains = gather_rows(grad_gains, BOTH).reshape(devices, -1, 128)[:, :lines]
+    grad_gains = lax.dynamic_slice_in_dim(
+        jnp.sum(grad_gains, axis=0).reshape(-1), lax.axis_index(BOTH) * gain_piece, gain_piece
+    )
+
+    columns = sum_rows(jnp.concatenate([grad_qkv, grad_mlp], axis=1), "dp")
+    columns = columns.reshape(ctx, rows, -1)
     columns = lax.all_to_all(columns, "ctx", 0, 0, tiled=True).transpose(1, 0, 2).astype(f32)
     own_qkv = columns[:, :, :qkv_width].reshape(rows, KEY_VALUE_HEADS, GROUP_WIDTH)
     own_mlp = columns[:, :, qkv_width:]
-    row_grads = lax.ppermute(jnp.concatenate([grad_out, grad_down], axis=0), BOTH, back)
+    row_grads = lax.ppermute(row_grads, BOTH, back)
     row_grads = row_grads.astype(f32)
     split = GROUPS * HEAD_SIZE
     return (

time: 912 us -> 673 us (0.74)
  waiting for transfers between devices: 668 us -> 385 us
  blocking collectives: 71.2 us -> 125 us
  matrix products: 62.8 us -> 48.2 us
    unnamed x18 -> x10, waiting for transfers between devices: 127 us -> 0.16 us
    reduce_scatter x8 -> x5, waiting for transfers between devices: 342 us -> 219 us  [sum_rows(): lax.psum_scatter(x.astype(bf16), axis, scatter_dimension=0, tiled=True)]
    all_gather x8 -> x5, waiting for transfers between devices: 199 us -> 158 us  [gather_rows(): return lax.all_gather(x, axis, axis=0, tiled=True)]
    all_gather x1 -> x2, blocking collectives: 52.9 us -> 87.3 us  [gather_rows(): return lax.all_gather(x, axis, axis=0, tiled=True)]
    all_to_all x1, blocking collectives: 18.3 us -> 37.8 us  [shards(): column_rows = lax.all_to_all(column_rows, 'ctx', 0, 0, tiled=True)]
  transfers between devices with their start and end apart: 20 -> 13, of which waited for: 16 -> 10; matrix products, arithmetic and copies ran while one was open for 8% -> 7% of each run, Pallas kernels for 4% -> 0%
where the time goes in v2:
time: 673 us; the launch traced here: 663 us
  waiting for transfers between devices  385 us (57%)
  blocking collectives  125 us (19%)
  matrix products  48.2 us (7%)
  Pallas kernels  35.9 us (5%)
  other arithmetic  27.2 us (4%)
  local copies, waits for them, and re-layouts  20.5 us (3%)
  between operations  15.1 us (2%)
  starting transfers between devices  6.75 us (1%)
    reduce_scatter x5, waiting for transfers between devices, sum_rows(): lax.psum_scatter(x.astype(bf16), axis, scatter_dimension=0, tiled=True)  219 us
    all_gather x5, waiting for transfers between devices, gather_rows(): return lax.all_gather(x, axis, axis=0, tiled=True)  158 us
    all_gather x2, blocking collectives, gather_rows(): return lax.all_gather(x, axis, axis=0, tiled=True)  87.3 us
    all_to_all x1, blocking collectives, shards(): column_rows = lax.all_to_all(column_rows, 'ctx', 0, 0, tiled=True)  37.8 us
    pallas_call x1, Pallas kernels, attention_backward(): pl.pallas_call(functools.partial(backward_kernel, 256), grid_spec=pltpu.P...  23.7 us
    dot_general x4, matrix products, dot_tn(): lax.dot_general(a, b, (((0,), (0,)), ((), ())), preferred_element_type=f32)  17.4 us
    dot_general x4, matrix products, dot_nt(): lax.dot_general(a, b, (((1,), (1,)), ((), ())), preferred_element_type=f32)  15.6 us
    dot_general x4, matrix products, dot_nn(): lax.dot_general(a, b, (((1,), (0,)), ((), ())), preferred_element_type=f32)  15.2 us
  transfers between devices with their start and end apart: 13, of which 10 were waited for; matrix products, arithmetic and copies ran while one was open for 7% of the time, Pallas kernels for 0%

profile of v2, /device:TPU:0, one launch (start us, length us, event | category | flops | bytes accessed | tf_op | source)
XLA Modules:
  0.0 663.3 jit_solution(778577804186144541)
XLA Ops:
  14.2 37.8 %all_to_all.10 = bf16[4,32,2560]{2,1,0:T(8,128)(2,1)} all-to-all(bf16[4,32,2560]{2,1,0:T(8,128)(2,1)S(1)} %copy.63), channel_id=1, replica_groups=mesh['dp'=8,'ctx'=4] {'ctx'}, dimensions={0} | all-to-all | bytes 1310720 | tf_op jit(solution)/shard_map/all_to_all | solution.py:298
  52.2 43.2 %all_gather.22 = bf16[512,128]{1,0:T(8,128)(2,1)S(1)} all-gather(bf16[16,128]{1,0:T(8,128)(2,1)S(1)} %pad.14), channel_id=1, replica_groups=mesh['dp'=8,'ctx'=4] {'dp','ctx'}, dimensions={0}, use_global_device_ids=true | all-gather | bytes 135168 | tf_op jit(solution)/shard_map/all_gather | solution.py:226
  100.4 28.9 %all-gather.6.cloned.1.call-done = bf16[1024,2048]{1,0:T(8,128)(2,1)} async-done(((bf16[256,2048]{1,0:T(8,128)(2,1)}), bf16[1024,2048]{1,0:T(8,128)(2,1)}) %all-gather.6.cloned.1.call-update) | async-done | bytes 4194320 | tf_op jit(solution)/shard_map/all_gather | solution.py:226
  131.4 86.4 %all-gather.8.cloned.1.call-done = bf16[1024,2560]{1,0:T(8,128)(2,1)} async-done(((bf16[128,2560]{1,0:T(8,128)(2,1)}), bf16[1024,2560]{1,0:T(8,128)(2,1)}) %all-gather.8.cloned.1.call-update) | async-done | bytes 5242896 | tf_op jit(solution)/shard_map/all_gather | solution.py:226
  217.8 4.6 fusion.16.raw_ref
  222.4 12.2 %shard_map.186 = bf16[1024,512]{1,0:T(8,128)(2,1)S(1)} custom-call(s32[8]{0:T(128)S(1)} %select_reduce_fusion.slot_ref, f32[1024,1024]{1,0:T(8,128)S(1)} %fusion.16.raw_ref, f32[1024,128]{1,0:T(8,128)S(1)} %get-tuple-element.37.cos_ref, f32[1024,128]{1,0:T(8,128)S(1)} %get-tuple-element.38.sin_ref, f32[8,128]{1,0:T(8,128)S(1)} %pad_convert_fusion.gains_ref), custom_call_target="tpu_custom_call" | custom-call | flops 2147483648 | bytes 4194304 | tf_op jit(solution)/shard_map/pallas_call | solution.py:167
  237.3 29.7 %reduce-scatter.6.cloned.1.call-done = bf16[256,1024]{1,0:T(8,128)(2,1)} async-done(((bf16[1024,1024]{1,0:T(8,128)(2,1)}), bf16[256,1024]{1,0:T(8,128)(2,1)}) %reduce-scatter.6.cloned.1.call-update) | async-done | bytes 524304 | tf_op jit(solution)/shard_map/reduce_scatter | solution.py:230
  273.4 19.7 %all-gather.12.cloned.1.call-done = bf16[1024,1024]{1,0:T(8,128)(2,1)} async-done(((bf16[256,1024]{1,0:T(8,128)(2,1)}), bf16[1024,1024]{1,0:T(8,128)(2,1)}) %all-gather.12.cloned.1.call-update) | async-done | bytes 2097168 | tf_op jit(solution)/shard_map/all_gather | solution.py:226
  293.2 6.1 fusion.6
  304.8 3.7 fusion.8
  311.1 44.6 %reduce-scatter.8.cloned.1.call-done = bf16[256,2048]{1,0:T(8,128)(2,1)} async-done(((bf16[1024,2048]{1,0:T(8,128)(2,1)}), bf16[256,2048]{1,0:T(8,128)(2,1)}) %reduce-scatter.8.cloned.1.call-update) | async-done | bytes 1048592 | tf_op jit(solution)/shard_map/reduce_scatter | solution.py:230
  359.9 22.7 %all-gather.14.cloned.1.call-done = bf16[1024,1024]{1,0:T(8,128)(2,1)} async-done(((bf16[256,1024]{1,0:T(8,128)(2,1)}), bf16[1024,1024]{1,0:T(8,128)(2,1)}) %all-gather.14.cloned.1.call-update) | async-done | bytes 2097168 | tf_op jit(solution)/shard_map/all_gather | solution.py:226
  385.9 23.7 %shard_map.187 = (bf16[1024,1024]{1,0:T(8,128)(2,1)S(1)}, f32[2,8,128]{2,1,0:T(8,128)S(1)}) custom-call(s32[8]{0:T(128)S(1)} %select_reduce_fusion.slot_ref, f32[1024,1024]{1,0:T(8,128)S(1)} %copy-done.1, f32[1024,128]{1,0:T(8,128)S(1)} %get-tuple-element.37.cos_ref, f32[1024,128]{1,0:T(8,128)S(1)} %get-tuple-element.38.sin_ref, ...), custom_call_target="tpu_custom_call" | custom-call | flops 5368709120 | bytes 6291456 | tf_op jit(solution)/shard_map/pallas_call | solution.py:195
  410.9 5.3 convolution_convert_fusion.2
  416.5 4.0 fusion.18
  423.6 8.2 %convolution_convert_fusion = bf16[1024,1536]{1,0:T(8,128)(2,1)} fusion(bf16[1024,1024]{1,0:T(8,128)(2,1)} %all-gather.12.cloned.1.call-done, bf16[1024,768]{0,1:T(8,128)(2,1)} %copy-done.24, bf16[1024,768]{0,1:T(8,128)(2,1)} %copy-done.23), kind=kOutput, calls=%fused_computation.7 | convolution fusion | flops 3229089792 | bytes 8388608 | tf_op jit(solution)/shard_map/dot_general | solution.py:39
  431.8 4.0 convolution_convert_fusion.1
  438.6 4.6 pad_maximum_fusion
  443.3 4.6 reduce-scatter.10.cloned.1.call-done
  452.3 70.0 %reduce-scatter.14.cloned.1.call-done = bf16[160,1024]{1,0:T(8,128)(2,1)} async-done(((bf16[1280,1024]{1,0:T(8,128)(2,1)}), bf16[160,1024]{1,0:T(8,128)(2,1)}) %reduce-scatter.14.cloned.1.call-update) | async-done | bytes 327696 | tf_op jit(solution)/shard_map/reduce_scatter | solution.py:230
  524.0 44.1 %all_gather.27 = f32[768,128]{1,0:T(8,128)S(1)} all-gather(f32[24,128]{1,0:T(8,128)S(1)} %pad.17), channel_id=1, replica_groups=mesh['dp'=8,'ctx'=4] {'dp','ctx'}, dimensions={0}, use_global_device_ids=true | all-gather | bytes 405504 | tf_op jit(solution)/shard_map/all_gather | solution.py:226
  568.0 69.8 %reduce-scatter.12.cloned.1.call-done = bf16[128,2560]{1,0:T(8,128)(2,1)} async-done(((bf16[1024,2560]{1,0:T(8,128)(2,1)}), bf16[128,2560]{1,0:T(8,128)(2,1)}) %reduce-scatter.12.cloned.1.call-update) | async-done | bytes 655376 | tf_op jit(solution)/shard_map/reduce_scatter | solution.py:230
  637.9 3.5 all-to-all-start.1
  643.7 7.9 %all-to-all-done.1 = bf16[4,32,2560]{2,1,0:T(8,128)(2,1)S(1)} async-done(((bf16[4,32,2560]{2,1,0:T(8,128)(2,1)}), bf16[4,32,2560]{2,1,0:T(8,128)(2,1)S(1)}, u32[]{:S(2)}, u32[]{:S(2)}) %all-to-all-start.1) | async-done | bytes 655392 | tf_op jit(solution)/shard_map/all_to_all | solution.py:375
  (151 shorter events, 58.9 us)
Async XLA Ops:
  7.2 6.2 copy-start.18
  7.2 6.2 copy-start.19
  7.2 90.9 %all-gather.10.cloned.1.call-start = ((), (), s32[]{:S(2)}) async-start(), calls=%async_computation.9 | async-start | bytes 2949120 | tf_op jit(solution)/shard_map/all_gather | solution.py:226
  9.3 0.8 collective-permute-start
  10.9 118.4 %all-gather.6.cloned.1.call-start = ((), (), s32[]{:S(2)}) async-start(), calls=%async_computation.7 | async-start | bytes 5242880 | tf_op jit(solution)/shard_map/all_gather | solution.py:226
  13.3 204.5 %all-gather.8.cloned.1.call-start = ((), (), s32[]{:S(2)}) async-start(), calls=%async_computation.8 | async-start | bytes 5898240 | tf_op jit(solution)/shard_map/all_gather | solution.py:226
  13.6 38.5 %copy-start.20 = (bf16[72]{0:T(256)(128)(2,1)S(1)}, bf16[72]{0:T(256)(128)(2,1)}, u32[]{:S(2)}) copy-start(bf16[72]{0:T(256)(128)(2,1)} %param.21) | copy-start | bytes 436
  13.7 81.9 %copy-start.21 = (s32[1,8]{1,0:T(1,128)S(1)}, s32[1,8]{1,0:T(1,128)}, u32[]{:S(2)}) copy-start(s32[1,8]{1,0:T(1,128)} %param.13) | copy-start | bytes 100
  52.1 215.0 %reduce-scatter.6.cloned.1.call-start = ((), (), s32[]{:S(2)}) async-start(), calls=%async_computation.10 | async-start | bytes 2621440 | tf_op jit(solution)/shard_map/reduce_scatter | solution.py:230
  222.4 12.3 %copy-start = (f32[1024,1024]{1,0:T(8,128)}, f32[1024,1024]{1,0:T(8,128)S(1)}, u32[]{:S(2)}) copy-start(f32[1024,1024]{1,0:T(8,128)S(1)} %fusion.16.raw_ref) | copy-start | bytes 12582916
  222.4 12.3 %copy-start.13 = (bf16[8,64,1024]{2,1,0:T(8,128)(2,1)S(1)}, bf16[8,64,1024]{2,1,0:T(8,128)(2,1)}, u32[]{:S(2)}) copy-start(bf16[8,64,1024]{2,1,0:T(8,128)(2,1)} %slice.106) | copy-start | bytes 3145732
  234.7 32.4 %copy-start.4 = (bf16[256,1024]{1,0:T(8,128)(2,1)S(1)}, bf16[256,1024]{1,0:T(8,128)(2,1)}, u32[]{:S(2)}) copy-start(bf16[256,1024]{1,0:T(8,128)(2,1)} %param.11) | copy-start | bytes 1572868
  237.3 55.9 %all-gather.12.cloned.1.call-start = ((), (), s32[]{:S(2)}) async-start(), calls=%async_computation.11 | async-start | bytes 2621440 | tf_op jit(solution)/shard_map/all_gather | solution.py:226
  270.4 85.3 %reduce-scatter.8.cloned.1.call-start = ((), (), s32[]{:S(2)}) async-start(), calls=%async_computation.12 | async-start | bytes 5242880 | tf_op jit(solution)/shard_map/reduce_scatter | solution.py:230
  293.2 11.6 %slice-start = ((s8[5242880]{0:T(1024)(128)(4,1)}), s8[4194304]{0:T(1024)(128)(4,1)S(1)}, s32[]{:S(2)}) async-start(s8[5242880]{0:T(1024)(128)(4,1)} %bitcast.77), calls=%async_computation.17 | async-start | bytes 8388608
  311.1 46.2 %copy-start.7 = (bf16[256,1024]{1,0:T(8,128)(2,1)S(1)}, bf16[256,1024]{1,0:T(8,128)(2,1)}, u32[]{:S(2)}) copy-start(bf16[256,1024]{1,0:T(8,128)(2,1)} %reduce-scatter.6.cloned.1.call-done) | copy-start | bytes 1572868
  311.1 71.6 %all-gather.14.cloned.1.call-start = ((), (), s32[]{:S(2)}) async-start(), calls=%async_computation.13 | async-start | bytes 2621440 | tf_op jit(solution)/shard_map/all_gather | solution.py:226
  359.9 88.0 %reduce-scatter.10.cloned.1.call-start = ((), (), s32[]{:S(2)}) async-start(), calls=%async_computation.14 | async-start | bytes 2621440 | tf_op jit(solution)/shard_map/reduce_scatter | solution.py:230
  416.3 106.1 %reduce-scatter.14.cloned.1.call-start = ((), (), s32[]{:S(2)}) async-start(), calls=%async_computation.16 | async-start | bytes 2949120 | tf_op jit(solution)/shard_map/reduce_scatter | solution.py:230
  423.5 8.2 %copy-start.3 = (bf16[1024,1024]{1,0:T(8,128)(2,1)S(1)}, bf16[1024,1024]{1,0:T(8,128)(2,1)}, u32[]{:S(2)}) copy-start(bf16[1024,1024]{1,0:T(8,128)(2,1)} %copy-done.2) | copy-start | bytes 6291460
  423.5 214.3 %reduce-scatter.12.cloned.1.call-start = ((), (), s32[]{:S(2)}) async-start(), calls=%async_computation.15 | async-start | bytes 5898240 | tf_op jit(solution)/shard_map/reduce_scatter | solution.py:230
  423.6 8.2 %copy-start.12 = (bf16[1024,2048]{1,0:T(8,128)(2,1)S(1)}, bf16[1024,2048]{1,0:T(8,128)(2,1)}, u32[]{:S(2)}) copy-start(bf16[1024,2048]{1,0:T(8,128)(2,1)} %all-gather.6.cloned.1.call-done) | copy-start | bytes 12582916
  522.3 119.7 %collective-permute-start.1 = (bf16[160,1024]{1,0:T(8,128)(2,1)}, bf16[160,1024]{1,0:T(8,128)(2,1)S(1)}, u32[]{:S(2)}, u32[]{:S(2)}) collective-permute-start(bf16[160,1024]{1,0:T(8,128)(2,1)} %reduce-scatter.14.cloned.1.call-done), channel_id=1, source_target_pairs={{0,0},{4,1},{8,2},{12,3},{16,4},{20,5},{24,6},{28,7},{1,8},{5,9},{... | collective-permute-start | bytes 983048 | tf_op jit(solution)/shard_map/ppermute | solution.py:378
  637.9 13.7 %all-to-all-start.1 = ((bf16[4,32,2560]{2,1,0:T(8,128)(2,1)}), bf16[4,32,2560]{2,1,0:T(8,128)(2,1)S(1)}, u32[]{:S(2)}, u32[]{:S(2)}) async-start(bf16[4,32,2560]{2,1,0:T(8,128)(2,1)} %bitcast.68), calls=%async_computation.5 | async-start | bytes 1310720 | tf_op jit(solution)/shard_map/all_to_all | solution.py:375
  (16 other events, 58.3 us)
Sparse Core Ops, SparseCore 0:
  11.0 82.9 all-gather.9
  96.2 33.0 all-gather.5
  131.5 86.2 all-gather.7
  237.4 29.5 reduce-scatter.5
  270.5 22.5 all-gather.11
  311.2 44.4 reduce-scatter.7
  360.0 22.5 all-gather.13
  416.4 31.4 reduce-scatter.9
  451.8 70.5 reduce-scatter.13
  526.2 111.6 reduce-scatter.11
